TPU v7x, 128 devices: a whole 4x4x4 slice. The times are simulated.
128 devices in a mesh: dp: 16 (over z_hi, x, core), head: 8 (over y, z_lo).
Axes of the slice: x: 4, y: 4, z: 4 (z_hi: 2, z_lo: 2; z = z_hi * 2 + z_lo), core: 2. Of those that a mesh axis runs over, the one named last changes fastest.
Arguments:
- tokens: bfloat16 [16384, 8192], P('dp'), may hold values from -64 to 64
- w_query: bfloat16 [8192, 8192], P('dp', 'head'), may hold values from -0.0625 to 0.0625
- key_weight: bfloat16 [8192, 1024], P('dp', 'head'), may hold values from -0.0625 to 0.0625
- value_weight: bfloat16 [8192, 1024], P('dp', 'head'), may hold values from -0.0625 to 0.0625
- segment_ids: int32 [16384], P('dp'), may hold values from 0 to 27, as said below
Outputs:
- attended: bfloat16 [16384, 8192], P('dp', 'head')
Inputs may be any that keep to these rules, and one draw needn't show every extreme that they name: `segment_ids`: within each sequence of 1024 tokens the numbers start at 0 and never fall.
All inputs are finite; a program needn't handle non-finite values.
Results may differ from a plain program's by a relative error of at most 0.01.
The roundings to bfloat16 on the way count: a program that leaves them out, or rounds other values in their place, can miss the bound.
Values may be sent and summed in bfloat16 or wider, within the bound.
A program may use at most 128 MiB of HBM per device.

v0:
```python
import jax
import jax.numpy as jnp
from jax import lax
from jax.sharding import PartitionSpec as P

QUERY_HEADS = 64
KEY_VALUE_HEADS = 8
HEAD_SIZE = 128
NBLK = 4


NEGATIVE = -1e30


def block_attend(queries, keys, values, segments, block):
    block_rows = queries.shape[0]
    heads_kv = queries.shape[1]
    grouped_heads = queries.shape[2]
    head_width = queries.shape[3]
    row_start = block * block_rows
    query_segments = segments[row_start : row_start + block_rows]
    query_positions = row_start + jnp.arange(block_rows, dtype=jnp.int32)
    inverse_root = 1.0 / jnp.sqrt(jnp.float32(head_width))

    def tile_update(state, column):
        running_max, denominator, weighted = state
        col_start = column * block_rows
        keys_tile = keys[col_start : col_start + block_rows]
        values_tile = values[col_start : col_start + block_rows]
        key_segments = segments[col_start : col_start + block_rows]
        key_positions = col_start + jnp.arange(block_rows, dtype=jnp.int32)
        mask = (key_positions[None, :] <= query_positions[:, None]) & (
            key_segments[None, :] == query_segments[:, None]
        )
        scores = (
            jnp.einsum("qhgd,khd->hgqk", queries, keys_tile, preferred_element_type=jnp.float32)
            * inverse_root
        )
        scores = jnp.where(mask, scores, NEGATIVE)
        new_max = jnp.maximum(running_max, jnp.max(scores, axis=3))
        weights = jnp.where(mask, jnp.exp(scores - new_max[..., None]), 0.0)
        fading = jnp.exp(running_max - new_max)
        denominator = denominator * fading + jnp.sum(weights, axis=3)
        weighted = weighted * fading[..., None] + jnp.einsum(
            "hgqk,khd->hgqd",
            weights.astype(jnp.bfloat16),
            values_tile,
            preferred_element_type=jnp.float32,
        )
        return (new_max, denominator, weighted)

    state = (
        jnp.full((heads_kv, grouped_heads, block_rows), NEGATIVE, jnp.float32),
        jnp.zeros((heads_kv, grouped_heads, block_rows), jnp.float32),
        jnp.zeros((heads_kv, grouped_heads, block_rows, head_width), jnp.float32),
    )
    for column in range(block + 1):
        if column == block:
            state = tile_update(state, column)
        else:
            needed = segments[row_start] == segments[column * block_rows + block_rows - 1]
            state = lax.cond(
                needed,
                lambda carried, column=column: tile_update(carried, column),
                lambda carried: carried,
                state,
            )
    result = state[2] / state[1][..., None]
    return (
        jnp.transpose(result, (2, 0, 1, 3))
        .reshape(block_rows, heads_kv * grouped_heads * head_width)
        .astype(jnp.bfloat16)
    )


def body(tokens, w_query, key_weight, value_weight, segment_ids):
    seq_rows = tokens.shape[0]

    def add_rows(piece):
        return jnp.dot(tokens, piece, preferred_element_type=jnp.float32)

    query_sum = add_rows(lax.all_gather(w_query, "dp", axis=0, tiled=True))
    key_sum = add_rows(lax.all_gather(key_weight, "dp", axis=0, tiled=True))
    value_sum = add_rows(lax.all_gather(value_weight, "dp", axis=0, tiled=True))
    heads_kv = key_weight.shape[1] // HEAD_SIZE
    grouped_heads = QUERY_HEADS // KEY_VALUE_HEADS
    queries = query_sum.astype(jnp.bfloat16).reshape(seq_rows, heads_kv, grouped_heads, HEAD_SIZE)
    keys = key_sum.astype(jnp.bfloat16).reshape(seq_rows, heads_kv, HEAD_SIZE)
    values = value_sum.astype(jnp.bfloat16).reshape(seq_rows, heads_kv, HEAD_SIZE)
    block_rows = seq_rows // NBLK
    pieces_out = [
        block_attend(
            queries[block * block_rows : (block + 1) * block_rows], keys, values, segment_ids, block
        )
        for block in range(NBLK)
    ]
    return jnp.concatenate(pieces_out, axis=0)


def solution(mesh):
    in_specs = (P("dp", None), P("dp", "head"), P("dp", "head"), P("dp", "head"), P("dp"))
    out_specs = P("dp", "head")
    return jax.shard_map(body, mesh=mesh, in_specs=in_specs, out_specs=out_specs, check_vma=False)
```

profile of v0, /device:TPU:3, one launch (start us, length us, event | category | flops | bytes accessed | tf_op | source)
XLA Modules:
  0.0 290.1 jit_solution(12813253240211798161)
XLA Ops:
  6.5 0.7 all-gather.4.cloned.1.call-update
  7.3 0.7 all-gather.8.cloned.1.call-update
  8.7 1.6 fusion.211
  17.8 0.8 fusion.210
  19.2 41.6 %all-gather.4.cloned.1.call-done = bf16[8192,128]{1,0:T(8,128)(2,1)} async-done(((bf16[512,128]{1,0:T(8,128)(2,1)}), bf16[8192,128]{1,0:T(8,128)(2,1)}) %all-gather.4.cloned.1.call-update) | async-done | bytes 2097168 | tf_op jit(solution)/shard_map/all_gather | solution.py:83
  60.8 10.8 %convolution_convert_fusion.2 = bf16[1024,128]{1,0:T(8,128)(2,1)S(1)} fusion(bf16[1024,8192]{1,0:T(8,128)(2,1)} %param.17, bf16[8192,128]{1,0:T(8,128)(2,1)} %all-gather.4.cloned.1.call-done), kind=kOutput, calls=%fused_computation.206 | convolution fusion | flops 2147614720 | bytes 19136512 | tf_op jit(solution)/shard_map/dot_general | solution.py:80
  71.7 38.7 %all-gather.8.cloned.1.call-done = bf16[8192,128]{1,0:T(8,128)(2,1)} async-done(((bf16[512,128]{1,0:T(8,128)(2,1)}), bf16[8192,128]{1,0:T(8,128)(2,1)}) %all-gather.8.cloned.1.call-update) | async-done | bytes 2097168 | tf_op jit(solution)/shard_map/all_gather | solution.py:84
  110.4 10.8 %convolution_convert_fusion.1 = bf16[1024,128]{1,0:T(8,128)(2,1)S(1)} fusion(bf16[1024,8192]{1,0:T(8,128)(2,1)} %param.17, bf16[8192,128]{1,0:T(8,128)(2,1)} %all-gather.8.cloned.1.call-done), kind=kOutput, calls=%fused_computation.205 | convolution fusion | flops 2147614720 | bytes 19136512 | tf_op jit(solution)/shard_map/dot_general | solution.py:80
  121.2 99.5 %all-gather.6.cloned.1.call-done = bf16[8192,1024]{1,0:T(8,128)(2,1)} async-done(((bf16[512,1024]{1,0:T(8,128)(2,1)}), bf16[8192,1024]{1,0:T(8,128)(2,1)}) %all-gather.6.cloned.1.call-update) | async-done | bytes 16777232 | tf_op jit(solution)/shard_map/all_gather | solution.py:82
  220.7 22.1 %convolution_convert_fusion = bf16[1024,1024]{0,1:T(8,128)(2,1)S(1)} fusion(bf16[1024,8192]{1,0:T(8,128)(2,1)} %param.17, bf16[8192,1024]{1,0:T(8,128)(2,1)} %all-gather.6.cloned.1.call-done), kind=kOutput, calls=%fused_computation.177 | convolution fusion | flops 17180917760 | bytes 35651584 | tf_op jit(solution)/shard_map/dot_general | solution.py:80
  244.6 1.0 copy.34
  245.6 2.0 conditional.7
  246.8 0.9 fusion.24
  247.6 5.0 %conditional.8 = (f32[1,8,256]{2,1,0:T(8,128)S(1)}, f32[1,8,256]{2,1,0:T(8,128)S(1)}, f32[1,8,256,128]{2,3,1,0:T(8,128)}) conditional(s32[]{:T(128)} %bitcast.98, (f32[1,8,256]{2,1,0:T(8,128)S(1)}, f32[1,8,256]{2,1,0:T(8,128)S(1)}, f32[1,8,256,128]{3,2,1,0:T(8,128)S(1)}) %conditional.7, (s32[256]{0:T(256)S(1)}, s32[1024]{0:T(1024)S(1)}, ...), branch_computations={%region_12.13_spmd, %region_13.16_spmd} | conditional | flops 275978496 | bytes 15735860 | solution.py:62
  248.3 1.8 fusion.46
  251.4 1.3 copy.65
  254.6 1.0 copy.36
  256.1 7.0 %conditional.6 = (f32[1,8,256]{2,1,0:T(8,128)S(1)}, f32[1,8,256]{2,1,0:T(8,128)}, f32[1,8,256,128]{2,3,1,0:T(8,128)}) conditional(s32[]{:T(128)} %bitcast.81, () %tuple.47, (s32[256]{0:T(256)S(1)}, s32[1024]{0:T(1024)S(1)}, s32[256]{0:T(256)S(1)}, bf16[1024,1,128]{2,0,1:T(8,128)(2,1)S(1)}, bf16[256,1024]{0,1:T(8,128)(2,1)S(1)}, ...), branch_computations={%region_2.3_spmd, %region_3.6_spmd} | conditional | flops 275720448 | bytes 10460184 | solution.py:62
  257.2 2.7 fusion.3
  259.9 2.5 copy.63
  263.6 0.7 fusion.190
  264.3 2.7 fusion.149
  267.0 1.2 copy.35
  268.3 2.9 conditional.9
  269.5 1.7 fusion.67
  271.2 3.1 %conditional.10 = ((f32[1,8,256]{2,1,0:T(8,128)S(1)}, f32[1,8,256]{2,1,0:T(8,128)S(1)}, f32[1,8,256,128]{3,2,1,0:T(8,128)S(1)})) conditional(s32[]{:T(128)} %bitcast.116, (f32[1,8,256]{2,1,0:T(8,128)S(1)}, f32[1,8,256]{2,1,0:T(8,128)S(1)}, f32[1,8,256,128]{3,2,1,0:T(8,128)S(1)}) %conditional.9, (s32[256]{0:T(256)S(1)}, s32[1024]{0:T(1024)S(1)}, ...), branch_computations={%region_22.23_spmd, %region_23.26_spmd} | conditional | flops 275978496 | bytes 9444384 | solution.py:62
  271.9 1.9 fusion.89
  274.3 4.5 %conditional.11 = (f32[1,8,256]{2,1,0:T(8,128)S(1)}, f32[1,8,256]{2,1,0:T(8,128)S(1)}, f32[1,8,256,128]{2,3,1,0:T(8,128)}) conditional(s32[]{:T(128)} %bitcast.115, (f32[1,8,256]{2,1,0:T(8,128)S(1)}, f32[1,8,256]{2,1,0:T(8,128)S(1)}, f32[1,8,256,128]{3,2,1,0:T(8,128)S(1)}) %get-tuple-element.352, (s32[256]{0:T(256)S(1)}, s32[1024]{0:T(1024)S(1)}, ...), branch_computations={%region_26.27_spmd, %region_27.30_spmd} | conditional | flops 275978496 | bytes 11541528 | solution.py:62
  275.2 1.7 fusion.110
  277.5 1.3 copy.67
  279.8 2.0 fusion.147
  282.1 1.5 pad_maximum_fusion
  (94 shorter events, 15.2 us)
Async XLA Ops:
  6.5 54.3 %all-gather.4.cloned.1.call-start = ((), (), s32[]{:S(2)}) async-start(), calls=%async_computation | async-start | bytes 2228224 | tf_op jit(solution)/shard_map/all_gather | solution.py:83
  7.3 103.1 %all-gather.8.cloned.1.call-start = ((), (), s32[]{:S(2)}) async-start(), calls=%async_computation.2 | async-start | bytes 2228224 | tf_op jit(solution)/shard_map/all_gather | solution.py:84
  8.0 212.7 %all-gather.6.cloned.1.call-start = ((), (), s32[]{:S(2)}) async-start(), calls=%async_computation.1 | async-start | bytes 17825792 | tf_op jit(solution)/shard_map/all_gather | solution.py:82
  17.7 1.3 copy-start.8
  18.6 0.6 copy-start.6
  121.2 132.5 %copy-start.10 = (bf16[1024,128]{1,0:T(8,128)(2,1)}, bf16[1024,128]{1,0:T(8,128)(2,1)S(1)}, u32[]{:S(2)}) copy-start(bf16[1024,128]{1,0:T(8,128)(2,1)S(1)} %convolution_convert_fusion.1) | copy-start | bytes 786436
  243.9 1.7 copy-start.4
  250.2 1.2 copy-start.2
  252.7 1.2 copy-start.3
  264.3 4.0 %copy-start.5 = (s32[1024]{0:T(1024)S(1)}, s32[1024]{0:T(1024)}, u32[]{:S(2)}) copy-start(s32[1024]{0:T(1024)} %param.21) | copy-start | bytes 12292
  264.3 4.0 %copy-start.7 = (s32[256]{0:T(256)S(1)}, s32[256]{0:T(256)}, u32[]{:S(2)}) copy-start(s32[256]{0:T(256)} %copy-done.6) | copy-start | bytes 3076
  264.3 4.0 %copy-start.9 = (s32[256]{0:T(256)S(1)}, s32[256]{0:T(256)}, u32[]{:S(2)}) copy-start(s32[256]{0:T(256)} %copy-done.8) | copy-start | bytes 3076
  279.8 2.2 copy-start
  279.8 2.2 copy-start.1
Sparse Core Ops, SparseCore 0:
  9.8 50.9 all-gather.3
  63.2 47.0 all-gather.7
  112.8 107.8 all-gather.5
where the time goes:
time: 291 us; the launch traced here: 290 us
  waiting for transfers between devices  182 us (63%)
  matrix products  65 us (22%)
  between operations  20.9 us (7%)
  local copies, waits for them, and re-layouts  12.3 us (4%)
  other arithmetic  9.28 us (3%)
    all_gather x1, waiting for transfers between devices, body(): query_sum = add_rows(lax.all_gather(w_query, 'dp', axis=0, tiled=True))  99.5 us
    dot_general x3, matrix products, add_rows(): return jnp.dot(tokens, piece, preferred_element_type=jnp.float32)  43.7 us
    all_gather x1, waiting for transfers between devices, body(): key_sum = add_rows(lax.all_gather(key_weight, 'dp', axis=0, tiled=True))  41.6 us
    all_gather x1, waiting for transfers between devices, body(): value_sum = add_rows(lax.all_gather(value_weight, 'dp', axis=0, tiled=True))  38.7 us
    dot_general x10, matrix products, tile_update(): jnp.einsum('hgqk,khd->hgqd', weights.astype(jnp.bfloat16), values_tile, p...  16.7 us
  transfers between devices with their start and end apart: 3, of which 3 were waited for; matrix products, arithmetic and copies ran while one was open for 8% of the time, Pallas kernels for 0%

commit v1 on v0

v1 whole, which is shorter than its diff:
```python
import functools
import math

import jax
import jax.numpy as jnp
from jax import lax
from jax.experimental import pallas as pl
from jax.experimental.pallas import tpu as pltpu
from jax.sharding import PartitionSpec as P

MESH = pl.DeviceIdType.MESH
HEAD = 128
PAIR = 2 * HEAD
NEGATIVE = -1e30
EXP2_SCALE = math.log2(math.e) / math.sqrt(HEAD)
LANE = 10
BLOCKS = 8
ROWS_X = 432
TILE = 256


def kernel(tok_hbm, wq_hbm, wk_hbm, wv_hbm, seg_ref, out_hbm,
           tok, w, acc, qkv, bias, outs,
           load_sem, tok_sem, out_sem, send_sem, recv_sem):
    tokens, width = tok.shape
    chunks = w.shape[0]
    rows = wq_hbm.shape[0]
    last = chunks - 1
    half = rows // 2
    me = lax.axis_index("dp")
    head = lax.axis_index("head")
    zh, x, core = me // 8, lax.rem(me // 2, 4), lax.rem(me, 2)

    def device(dz, dx, dc):
        return (lax.rem(zh + dz, 2) * 4 + lax.rem(x + dx, 4)) * 2 + lax.rem(core + dc, 2)

    OWN, XP, XM, X2, ZO, PP, PM, CO = (0, 0), (0, 1), (0, 3), (0, 2), (1, 0), (1, 1), (1, 3), (1, 2)
    ORDER = (OWN, XP, XM, X2, ZO, PP, PM, CO)
    to_left, to_right = (device(0, 3, 0), head), (device(0, 1, 0), head)
    partner, sibling = (device(1, 0, 0), head), (device(0, 0, 1), head)

    def part(c, pos, dc, first, count):
        start = pl.multiple_of(device(pos[0], pos[1], dc) * rows + first, 16)
        return w.at[c, pl.ds(start, count)]

    def send(c, pos, first, count, target, slot):
        ref = part(c, pos, 0, first, count)
        pltpu.make_async_remote_copy(
            src_ref=ref, dst_ref=ref, send_sem=send_sem.at[c, slot], recv_sem=recv_sem.at[c, slot],
            device_id=target, device_id_type=MESH).start()

    def pair(c, pos):
        send(c, pos, 0, rows, sibling, LANE + ORDER.index(pos))

    def wait(c, pos, first, count, slot, dc=0):
        ref = part(c, pos, dc, first, count)
        pltpu.make_async_remote_copy(
            src_ref=ref, dst_ref=ref, send_sem=send_sem.at[c, slot], recv_sem=recv_sem.at[c, slot],
            device_id=sibling, device_id_type=MESH).wait_recv()

    def send_own(c):
        send(c, OWN, 0, rows, to_left, 0)
        send(c, OWN, 0, rows, to_right, 1)
        send(c, OWN, 0, rows, partner, 6)
        pair(c, OWN)

    def take_x(c):
        wait(c, XP, 0, rows, 0)
        wait(c, XM, 0, rows, 1)
        if ROWS_X < rows:
            send(c, XP, ROWS_X, rows - ROWS_X, partner, 8)
            send(c, XM, ROWS_X, rows - ROWS_X, partner, 9)
        pair(c, XP)
        pair(c, XM)

    def send_halves(c):
        send(c, XP, 0, half, to_left, 2)
        send(c, XM, half, half, to_right, 3)

    def take_z(c):
        wait(c, ZO, 0, rows, 6)
        send(c, ZO, 0, ROWS_X, to_left, 4)
        send(c, ZO, 0, ROWS_X, to_right, 5)
        pair(c, ZO)

    def take_halves(c):
        wait(c, X2, 0, half, 2)
        wait(c, X2, half, half, 3)
        send(c, X2, 0, rows, partner, 7)
        pair(c, X2)

    def take_far(c):
        wait(c, PP, 0, ROWS_X, 4)
        wait(c, PM, 0, ROWS_X, 5)
        if ROWS_X < rows:
            wait(c, PP, ROWS_X, rows - ROWS_X, 8)
            wait(c, PM, ROWS_X, rows - ROWS_X, 9)
        pair(c, PP)
        pair(c, PM)

    def take_corner(c):
        wait(c, CO, 0, rows, 7)
        pair(c, CO)

    def take_siblings(c):
        for i, pos in enumerate(ORDER):
            wait(c, pos, 0, rows, LANE + i, dc=1)

    def project(c, pos, first=False):
        start = pl.multiple_of((lax.rem(zh + pos[0], 2) * 4 + lax.rem(x + pos[1], 4)) * 2 * rows, 1024)

        def tile(i, carry):
            at = pl.ds(pl.multiple_of(i * 512, 512), 512)
            part_sum = jnp.dot(tok[at, pl.ds(start, 2 * rows)], w[c, pl.ds(start, 2 * rows)],
                               preferred_element_type=jnp.float32)
            acc[at] = part_sum if first else acc[at] + part_sum
            return carry

        lax.fori_loop(0, tokens // 512, tile, 0)

    def round_chunk(c):
        for h in range(2):
            qkv[c, h] = acc[:, h * HEAD:(h + 1) * HEAD].astype(jnp.bfloat16)

    def attend(c, h):
        for i in range(tokens // TILE):
            n = (i + 1) * TILE
            at = slice(i * TILE, n)
            s = lax.dot_general(qkv[c, h, at], qkv[0, 0, :n], (((1,), (1,)), ((), ())),
                                preferred_element_type=jnp.float32)
            s = s + bias[at, :n]
            p = jnp.exp2((s - jnp.max(s, axis=1, keepdims=True)) * EXP2_SCALE)
            total = jnp.sum(p, axis=1, keepdims=True)
            o = jnp.dot(p.astype(jnp.bfloat16), qkv[0, 1, :n], preferred_element_type=jnp.float32)
            outs[(c - 1) * 2 + h, at] = (o / total).astype(jnp.bfloat16)
        out_copy(c, h).start()

    def out_copy(c, h):
        j = (c - 1) * 2 + h
        return pltpu.make_async_copy(
            outs.at[j], out_hbm.at[:, pl.ds(pl.multiple_of(j * HEAD, HEAD), HEAD)], out_sem.at[j])

    def loads(c):
        at = pl.ds(pl.multiple_of(me * rows, rows), rows)
        if c == 0:
            return [pltpu.make_async_copy(wk_hbm, w.at[0, at, pl.ds(0, HEAD)], load_sem.at[0]),
                    pltpu.make_async_copy(wv_hbm, w.at[0, at, pl.ds(HEAD, HEAD)], load_sem.at[chunks])]
        return [pltpu.make_async_copy(wq_hbm.at[:, pl.ds((c - 1) * PAIR, PAIR)], w.at[c, at], load_sem.at[c])]

    for c in range(chunks):
        for copy in loads(c):
            copy.start()
    tok_copy = pltpu.make_async_copy(tok_hbm, tok, tok_sem)
    tok_copy.start()

    barrier = pltpu.get_barrier_semaphore()
    for target in (to_left, to_right, partner, sibling):
        pl.semaphore_signal(barrier, inc=1, device_id=target, device_id_type=MESH)
    pl.semaphore_wait(barrier, 4)

    for c in range(chunks):
        for copy in loads(c):
            copy.wait()
        if c < 2:
            send_own(c)

    for i in range(tokens // HEAD):
        mine = jnp.transpose(jnp.broadcast_to(seg_ref[i:i + 1, :], (HEAD, HEAD)))
        for j in range((i * HEAD // TILE + 1) * TILE // HEAD):
            ok = mine == jnp.broadcast_to(seg_ref[j:j + 1, :], (HEAD, HEAD))
            t = lax.broadcasted_iota(jnp.int32, (HEAD, HEAD), 0) + i * HEAD
            u = lax.broadcasted_iota(jnp.int32, (HEAD, HEAD), 1) + j * HEAD
            bias[i * HEAD:(i + 1) * HEAD, j * HEAD:(j + 1) * HEAD] = jnp.where(
                jnp.logical_and(ok, u <= t), jnp.float32(0.0), jnp.float32(NEGATIVE))

    take_x(0)
    send_halves(0)
    tok_copy.wait()

    def body(c, carry):
        @pl.when(c < last)
        def _():
            take_x(c + 1)

        take_z(c)

        @pl.when(c > 0)
        def _():
            project(c - 1, OWN, first=True)
            for pos in (XP, XM, X2):
                project(c - 1, pos)

        take_halves(c)

        @pl.when(c < last - 1)
        def _():
            send_own(c + 2)

        @pl.when(c > 0)
        def _():
            for pos in (ZO, PP, PM, CO):
                project(c - 1, pos)
            round_chunk(c - 1)

        take_far(c)

        @pl.when(c < last)
        def _():
            send_halves(c + 1)

        @pl.when(c > 1)
        def _():
            attend(c - 1, 0)

        take_corner(c)

        @pl.when(c > 1)
        def _():
            attend(c - 1, 1)

        take_siblings(c)
        return carry

    lax.fori_loop(0, chunks, body, 0)

    project(last, OWN, first=True)
    for pos in ORDER[1:]:
        project(last, pos)
    round_chunk(last)
    attend(last, 0)
    attend(last, 1)

    def drain(c, carry):
        for slot, (pos, first, count) in enumerate(
                ((OWN, 0, rows), (OWN, 0, rows), (XP, 0, half), (XM, half, half), (ZO, 0, ROWS_X), (ZO, 0, ROWS_X),
                 (OWN, 0, rows), (X2, 0, rows), (XP, ROWS_X, rows - ROWS_X), (XM, ROWS_X, rows - ROWS_X))
                + tuple((pos, 0, rows) for pos in ORDER)):
            if count > 0:
                ref = part(c, pos, 0, first, count)
                pltpu.make_async_remote_copy(
                    src_ref=ref, dst_ref=ref, send_sem=send_sem.at[c, slot], recv_sem=recv_sem.at[c, slot],
                    device_id=sibling, device_id_type=MESH).wait_send()
        return carry

    lax.fori_loop(0, chunks, drain, 0)

    def drain_out(c, carry):
        for h in range(2):
            out_copy(c, h).wait()
        return carry

    lax.fori_loop(1, chunks, drain_out, 0)


def body(tokens, w_query, key_weight, value_weight, segment_ids):
    seq, width = tokens.shape
    rows, columns = w_query.shape
    chunks = columns // PAIR + 1
    heads = columns // HEAD
    any_space = pl.BlockSpec(memory_space=pl.ANY)
    flops = 2 * seq * width * (columns + PAIR)
    return pl.pallas_call(
        kernel,
        out_shape=jax.ShapeDtypeStruct((seq, columns), jnp.bfloat16),
        in_specs=[any_space] * 4 + [pl.BlockSpec(memory_space=pltpu.VMEM)],
        out_specs=any_space,
        scratch_shapes=[
            pltpu.VMEM((seq, width), jnp.bfloat16),
            pltpu.VMEM((chunks, width, PAIR), jnp.bfloat16),
            pltpu.VMEM((seq, PAIR), jnp.float32),
            pltpu.VMEM((chunks, 2, seq, HEAD), jnp.bfloat16),
            pltpu.VMEM((seq, seq), jnp.float32),
            pltpu.VMEM((heads, seq, HEAD), jnp.bfloat16),
            pltpu.SemaphoreType.DMA((chunks + 1,)),
            pltpu.SemaphoreType.DMA,
            pltpu.SemaphoreType.DMA((heads,)),
            pltpu.SemaphoreType.DMA((chunks, LANE + BLOCKS)),
            pltpu.SemaphoreType.DMA((chunks, LANE + BLOCKS)),
        ],
        compiler_params=pltpu.CompilerParams(
            collective_id=0, has_side_effects=True, vmem_limit_bytes=58 * 2**20),
        cost_estimate=pl.CostEstimate(flops=flops, bytes_accessed=40 * 2**20, transcendentals=8 * seq * seq),
    )(tokens, w_query, key_weight, value_weight, segment_ids.reshape(seq // HEAD, HEAD))


def solution(mesh):
    in_specs = (P("dp", None), P("dp", "head"), P("dp", "head"), P("dp", "head"), P("dp"))
    return jax.shard_map(body, mesh=mesh, in_specs=in_specs, out_specs=P("dp", "head"), check_vma=False)
```

time: 291 us -> 108 us (0.37)
  the two profiles are of different devices: /device:TPU:3 before, /device:TPU:1 now
where the time goes in v1:
time: 108 us
  Pallas kernels  105 us (97%)
  local copies, waits for them, and re-layouts  3.08 us (3%)
    pallas_call x1, Pallas kernels, body(): pl.pallas_call(kernel, out_shape=jax.ShapeDtypeStruct((seq, columns), jnp...  105 us
    unnamed x1, local copies, waits for them, and re-layouts  3.08 us

profile of v1, /device:TPU:1, one launch (start us, length us, event | category | flops | bytes accessed | tf_op | source)
XLA Modules:
  0.0 107.9 jit_solution(3508430286935070695)
XLA Ops:
  0.0 104.8 %shard_map.55 = bf16[1024,1024]{1,0:T(8,128)(2,1)} custom-call(bf16[1024,8192]{1,0:T(8,128)(2,1)} %tok_hbm.1, bf16[512,1024]{1,0:T(8,128)(2,1)} %wq_hbm.1, bf16[512,128]{1,0:T(8,128)(2,1)} %wk_hbm.1, bf16[512,128]{1,0:T(8,128)(2,1)} %wv_hbm.1, s32[8,128]{1,0:T(8,128)} %bitcast.1), custom_call_target="tpu_custom_call" | custom-call | flops 21474836480 | bytes 41943040 | tf_op jit(solution)/shard_map/pallas_call | solution.py:262
  104.8 3.1 %copy.7 = bf16[1024,1024]{1,0:T(8,128)(2,1)} copy(bf16[1024,1024]{1,0:T(8,128)(2,1)} %shard_map.55) | data formatting | bytes 4194304

commit v2 on v1

--- a/solution.py
+++ b/solution.py
@@ -17,6 +17,25 @@
 BLOCKS = 8
 ROWS_X = 432
 TILE = 256
+
+ORDER = (
+    ("own", 0), ("own", 1), ("mul", 0, "OWN"), ("own", 2), ("x", 0), ("z", 0), ("mul", 0, "XP"),
+    ("mul", 0, "XM"), ("mul", 0, "ZO"), ("x", 1), ("z", 1), ("x", 2), ("z", 2), ("halves", 0),
+    ("mul", 0, "X2"), ("far", 0), ("halves", 1), ("far", 1), ("halves", 2), ("corner", 0), ("own", 3),
+    ("mul", 0, "CO"), ("take_far", 0), ("mul", 0, "PP"), ("mul", 0, "PM"), ("corner", 1), ("round", 0),
+    ("far", 2), ("mul", 1, "OWN"), ("mul", 1, "XP"), ("take_far", 1), ("mul", 1, "XM"), ("mul", 1, "ZO"),
+    ("mul", 1, "X2"), ("mul", 1, "CO"), ("mul", 1, "PP"), ("mul", 1, "PM"), ("round", 1), ("attend", 1, 0),
+    ("corner", 2), ("own", 4), ("attend", 1, 1), ("attend", 1, 2), ("x", 3), ("attend", 1, 3),
+    ("mul", 2, "OWN"), ("mul", 2, "XP"), ("mul", 2, "XM"), ("mul", 2, "ZO"), ("mul", 2, "X2"),
+    ("mul", 2, "CO"), ("z", 3), ("take_far", 2), ("mul", 2, "PP"), ("mul", 2, "PM"), ("round", 2),
+    ("attend", 2, 0), ("far", 3), ("attend", 2, 1), ("z", 4), ("attend", 2, 2), ("x", 4), ("attend", 2, 3),
+    ("mul", 3, "OWN"), ("mul", 3, "XP"), ("mul", 3, "XM"), ("halves", 3), ("mul", 3, "ZO"), ("mul", 3, "X2"),
+    ("far", 4), ("take_far", 3), ("corner", 3), ("mul", 3, "PP"), ("halves", 4), ("mul", 3, "PM"),
+    ("mul", 3, "CO"), ("round", 3), ("attend", 3, 0), ("attend", 3, 1), ("attend", 3, 2), ("attend", 3, 3),
+    ("mul", 4, "OWN"), ("mul", 4, "XP"), ("take_far", 4), ("mul", 4, "XM"), ("mul", 4, "ZO"), ("mul", 4, "X2"),
+    ("corner", 4), ("mul", 4, "PP"), ("mul", 4, "PM"), ("mul", 4, "CO"), ("round", 4), ("attend", 4, 0),
+    ("attend", 4, 1), ("attend", 4, 2), ("attend", 4, 3),
+)
 
 
 def kernel(tok_hbm, wq_hbm, wk_hbm, wv_hbm, seg_ref, out_hbm,
@@ -35,7 +54,8 @@
         return (lax.rem(zh + dz, 2) * 4 + lax.rem(x + dx, 4)) * 2 + lax.rem(core + dc, 2)
 
     OWN, XP, XM, X2, ZO, PP, PM, CO = (0, 0), (0, 1), (0, 3), (0, 2), (1, 0), (1, 1), (1, 3), (1, 2)
-    ORDER = (OWN, XP, XM, X2, ZO, PP, PM, CO)
+    ALL = (OWN, XP, XM, X2, ZO, PP, PM, CO)
+    BY_NAME = dict(OWN=OWN, XP=XP, XM=XM, X2=X2, ZO=ZO, PP=PP, PM=PM, CO=CO)
     to_left, to_right = (device(0, 3, 0), head), (device(0, 1, 0), head)
     partner, sibling = (device(1, 0, 0), head), (device(0, 0, 1), head)
 
@@ -50,7 +70,7 @@
             device_id=target, device_id_type=MESH).start()
 
     def pair(c, pos):
-        send(c, pos, 0, rows, sibling, LANE + ORDER.index(pos))
+        send(c, pos, 0, rows, sibling, LANE + ALL.index(pos))
 
     def wait(c, pos, first, count, slot, dc=0):
         ref = part(c, pos, dc, first, count)
@@ -66,22 +86,22 @@
 
     def take_x(c):
         wait(c, XP, 0, rows, 0)
+        send(c, XP, 0, half, to_left, 2)
         wait(c, XM, 0, rows, 1)
+        send(c, XM, half, half, to_right, 3)
         if ROWS_X < rows:
             send(c, XP, ROWS_X, rows - ROWS_X, partner, 8)
             send(c, XM, ROWS_X, rows - ROWS_X, partner, 9)
         pair(c, XP)
         pair(c, XM)
 
-    def send_halves(c):
-        send(c, XP, 0, half, to_left, 2)
-        send(c, XM, half, half, to_right, 3)
-
     def take_z(c):
         wait(c, ZO, 0, rows, 6)
+        pair(c, ZO)
+
+    def send_far(c):
         send(c, ZO, 0, ROWS_X, to_left, 4)
         send(c, ZO, 0, ROWS_X, to_right, 5)
-        pair(c, ZO)
 
     def take_halves(c):
         wait(c, X2, 0, half, 2)
@@ -102,38 +122,42 @@
         wait(c, CO, 0, rows, 7)
         pair(c, CO)
 
-    def take_siblings(c):
-        for i, pos in enumerate(ORDER):
-            wait(c, pos, 0, rows, LANE + i, dc=1)
-
-    def project(c, pos, first=False):
+    started = set()
+
+    def project(c, name):
+        pos = BY_NAME[name]
+        wait(c, pos, 0, rows, LANE + ALL.index(pos), dc=1)
         start = pl.multiple_of((lax.rem(zh + pos[0], 2) * 4 + lax.rem(x + pos[1], 4)) * 2 * rows, 1024)
-
-        def tile(i, carry):
-            at = pl.ds(pl.multiple_of(i * 512, 512), 512)
-            part_sum = jnp.dot(tok[at, pl.ds(start, 2 * rows)], w[c, pl.ds(start, 2 * rows)],
+        first = c not in started
+        started.add(c)
+        def go():
+            part_sum = jnp.dot(tok[:, pl.ds(start, 2 * rows)], w[c, pl.ds(start, 2 * rows)],
                                preferred_element_type=jnp.float32)
-            acc[at] = part_sum if first else acc[at] + part_sum
-            return carry
-
-        lax.fori_loop(0, tokens // 512, tile, 0)
+            acc[...] = part_sum if first else acc[...] + part_sum
+        pl.when(me >= 0)(go)
 
     def round_chunk(c):
-        for h in range(2):
-            qkv[c, h] = acc[:, h * HEAD:(h + 1) * HEAD].astype(jnp.bfloat16)
-
-    def attend(c, h):
-        for i in range(tokens // TILE):
-            n = (i + 1) * TILE
-            at = slice(i * TILE, n)
-            s = lax.dot_general(qkv[c, h, at], qkv[0, 0, :n], (((1,), (1,)), ((), ())),
-                                preferred_element_type=jnp.float32)
-            s = s + bias[at, :n]
-            p = jnp.exp2((s - jnp.max(s, axis=1, keepdims=True)) * EXP2_SCALE)
+        def go():
+            for h in range(2):
+                qkv[c, h] = acc[:, h * HEAD:(h + 1) * HEAD].astype(jnp.bfloat16)
+        pl.when(me >= 0)(go)
+
+    def attend(c, i):
+        pl.when(me >= 0)(functools.partial(attend_in, c, i))
+
+    def attend_in(c, i):
+        n = (i + 1) * TILE
+        at = slice(i * TILE, n)
+        scores = [lax.dot_general(qkv[c, h, at], qkv[0, 0, :n], (((1,), (1,)), ((), ())),
+                                  preferred_element_type=jnp.float32) + bias[at, :n] for h in range(2)]
+        weights = [jnp.exp2((s - jnp.max(s, axis=1, keepdims=True)) * EXP2_SCALE) for s in scores]
+        for h, p in enumerate(weights):
             total = jnp.sum(p, axis=1, keepdims=True)
             o = jnp.dot(p.astype(jnp.bfloat16), qkv[0, 1, :n], preferred_element_type=jnp.float32)
             outs[(c - 1) * 2 + h, at] = (o / total).astype(jnp.bfloat16)
-        out_copy(c, h).start()
+        if i == tokens // TILE - 1:
+            for h in range(2):
+                out_copy(c, h).start()
 
     def out_copy(c, h):
         j = (c - 1) * 2 + h
@@ -150,19 +174,30 @@
     for c in range(chunks):
         for copy in loads(c):
             copy.start()
-    tok_copy = pltpu.make_async_copy(tok_hbm, tok, tok_sem)
-    tok_copy.start()
+
+    def tok_copy(name):
+        pos = BY_NAME[name]
+        start = pl.multiple_of((lax.rem(zh + pos[0], 2) * 4 + lax.rem(x + pos[1], 4)) * 2 * rows, 1024)
+        at = pl.ds(start, 2 * rows)
+        return pltpu.make_async_copy(tok_hbm.at[:, at], tok.at[:, at], tok_sem.at[ALL.index(pos)])
 
     barrier = pltpu.get_barrier_semaphore()
     for target in (to_left, to_right, partner, sibling):
         pl.semaphore_signal(barrier, inc=1, device_id=target, device_id_type=MESH)
     pl.semaphore_wait(barrier, 4)
 
-    for c in range(chunks):
+    head_count = 0
+    while ORDER[head_count][0] == "own":
+        for copy in loads(ORDER[head_count][1]):
+            copy.wait()
+        send_own(ORDER[head_count][1])
+        head_count += 1
+    for c in range(head_count, chunks):
         for copy in loads(c):
             copy.wait()
-        if c < 2:
-            send_own(c)
+
+    for name in BY_NAME:
+        tok_copy(name).start()
 
     for i in range(tokens // HEAD):
         mine = jnp.transpose(jnp.broadcast_to(seg_ref[i:i + 1, :], (HEAD, HEAD)))
@@ -173,68 +208,20 @@
             bias[i * HEAD:(i + 1) * HEAD, j * HEAD:(j + 1) * HEAD] = jnp.where(
                 jnp.logical_and(ok, u <= t), jnp.float32(0.0), jnp.float32(NEGATIVE))
 
-    take_x(0)
-    send_halves(0)
-    tok_copy.wait()
-
-    def body(c, carry):
-        @pl.when(c < last)
-        def _():
-            take_x(c + 1)
-
-        take_z(c)
-
-        @pl.when(c > 0)
-        def _():
-            project(c - 1, OWN, first=True)
-            for pos in (XP, XM, X2):
-                project(c - 1, pos)
-
-        take_halves(c)
-
-        @pl.when(c < last - 1)
-        def _():
-            send_own(c + 2)
-
-        @pl.when(c > 0)
-        def _():
-            for pos in (ZO, PP, PM, CO):
-                project(c - 1, pos)
-            round_chunk(c - 1)
-
-        take_far(c)
-
-        @pl.when(c < last)
-        def _():
-            send_halves(c + 1)
-
-        @pl.when(c > 1)
-        def _():
-            attend(c - 1, 0)
-
-        take_corner(c)
-
-        @pl.when(c > 1)
-        def _():
-            attend(c - 1, 1)
-
-        take_siblings(c)
-        return carry
-
-    lax.fori_loop(0, chunks, body, 0)
-
-    project(last, OWN, first=True)
-    for pos in ORDER[1:]:
-        project(last, pos)
-    round_chunk(last)
-    attend(last, 0)
-    attend(last, 1)
+    steps = dict(own=send_own, x=take_x, z=take_z, far=send_far, halves=take_halves, take_far=take_far, corner=take_corner,
+                 mul=project, round=round_chunk, attend=attend)
+    seen = set()
+    for step in ORDER[head_count:]:
+        if step[0] == "mul" and step[2] not in seen:
+            tok_copy(step[2]).wait()
+            seen.add(step[2])
+        steps[step[0]](*step[1:])
 
     def drain(c, carry):
         for slot, (pos, first, count) in enumerate(
                 ((OWN, 0, rows), (OWN, 0, rows), (XP, 0, half), (XM, half, half), (ZO, 0, ROWS_X), (ZO, 0, ROWS_X),
                  (OWN, 0, rows), (X2, 0, rows), (XP, ROWS_X, rows - ROWS_X), (XM, ROWS_X, rows - ROWS_X))
-                + tuple((pos, 0, rows) for pos in ORDER)):
+                + tuple((pos, 0, rows) for pos in ALL)):
             if count > 0:
                 ref = part(c, pos, 0, first, count)
                 pltpu.make_async_remote_copy(
@@ -272,7 +259,7 @@
             pltpu.VMEM((seq, seq), jnp.float32),
             pltpu.VMEM((heads, seq, HEAD), jnp.bfloat16),
             pltpu.SemaphoreType.DMA((chunks + 1,)),
-            pltpu.SemaphoreType.DMA,
+            pltpu.SemaphoreType.DMA((8,)),
             pltpu.SemaphoreType.DMA((heads,)),
             pltpu.SemaphoreType.DMA((chunks, LANE + BLOCKS)),
             pltpu.SemaphoreType.DMA((chunks, LANE + BLOCKS)),

time: 108 us -> 92.7 us (0.86)
  Pallas kernels: 105 us -> 89.5 us
    pallas_call x1, Pallas kernels: 105 us -> 89.5 us  [body(): pl.pallas_call(kernel, out_shape=jax.ShapeDtypeStruct((seq, columns), jnp...]
where the time goes in v2:
time: 92.7 us; the launch traced here: 92.6 us
  Pallas kernels  89.5 us (97%)
  local copies, waits for them, and re-layouts  3.08 us (3%)
    pallas_call x1, Pallas kernels, body(): pl.pallas_call(kernel, out_shape=jax.ShapeDtypeStruct((seq, columns), jnp...  89.5 us
    unnamed x1, local copies, waits for them, and re-layouts  3.08 us

profile of v2, /device:TPU:1, one launch (start us, length us, event | category | flops | bytes accessed | tf_op | source)
XLA Modules:
  0.0 92.6 jit_solution(6856825710928480669)
XLA Ops:
  0.0 89.5 %shard_map.55 = bf16[1024,1024]{1,0:T(8,128)(2,1)} custom-call(bf16[1024,8192]{1,0:T(8,128)(2,1)} %tok_hbm.1, bf16[512,1024]{1,0:T(8,128)(2,1)} %wq_hbm.1, bf16[512,128]{1,0:T(8,128)(2,1)} %wk_hbm.1, bf16[512,128]{1,0:T(8,128)(2,1)} %wv_hbm.1, s32[8,128]{1,0:T(8,128)} %bitcast.1), custom_call_target="tpu_custom_call" | custom-call | flops 21474836480 | bytes 41943040 | tf_op jit(solution)/shard_map/pallas_call | solution.py:249
  89.5 3.1 %copy.7 = bf16[1024,1024]{1,0:T(8,128)(2,1)} copy(bf16[1024,1024]{1,0:T(8,128)(2,1)} %shard_map.55) | data formatting | bytes 4194304

commit v3 on v2

v3 whole, which is shorter than its diff:
```python
import functools
import math

import jax
import jax.numpy as jnp
from jax import lax
from jax.experimental import pallas as pl
from jax.experimental.pallas import tpu as pltpu
from jax.sharding import PartitionSpec as P

MESH = pl.DeviceIdType.MESH
HEAD = 128
NEGATIVE = -1e30
EXP2_SCALE = math.log2(math.e) / math.sqrt(HEAD)
LANE = 14
BLOCKS = 8
ROWS_X = (416, 416, 416, 416, 416)
PIECES = (1, 1, 1, 1, 1)
MUL_RUN = 2
TILE_RUN = 4
TILE = 256

CHUNKS = ((0, 2), (2, 2), (4, 2), (6, 2), (8, 2))

ORDER = (
    ("own", 0), ("own", 1), ("own", 2), ("mul", 0, "OWN"), ("mul", 1, "OWN"), ("own", 3), ("x", 0), ("z", 0),
    ("mul", 0, "XP"), ("mul", 0, "XM"), ("mul", 0, "ZO"), ("x", 1), ("z", 1), ("mul", 1, "XP"),
    ("mul", 1, "XM"), ("mul", 1, "ZO"), ("x", 2), ("z", 2), ("x", 3), ("z", 3), ("halves", 0),
    ("mul", 0, "X2"), ("far", 0), ("halves", 1), ("mul", 1, "X2"), ("far", 1), ("halves", 2), ("far", 2),
    ("halves", 3), ("corner", 0), ("own", 4), ("take_far", 0), ("mul", 0, "CO"), ("mul", 0, "PP"),
    ("mul", 0, "PM"), ("far", 3), ("corner", 1), ("round", 0), ("mul", 2, "OWN"), ("take_far", 1),
    ("mul", 2, "XP"), ("mul", 2, "XM"), ("mul", 1, "CO"), ("mul", 2, "ZO"), ("mul", 2, "X2"), ("mul", 1, "PP"),
    ("mul", 1, "PM"), ("take_far", 2), ("round", 1), ("corner", 2), ("attend", 1, 0), ("attend", 1, 1),
    ("attend", 1, 2), ("attend", 1, 3), ("mul", 2, "PP"), ("mul", 2, "CO"), ("mul", 2, "PM"), ("round", 2),
    ("attend", 2, 0), ("attend", 2, 1), ("x", 4), ("corner", 3), ("attend", 2, 2), ("attend", 2, 3),
    ("mul", 3, "OWN"), ("mul", 3, "XP"), ("mul", 3, "XM"), ("mul", 3, "ZO"), ("take_far", 3), ("mul", 3, "X2"),
    ("mul", 3, "CO"), ("z", 4), ("far", 4), ("mul", 4, "OWN"), ("mul", 4, "XP"), ("halves", 4),
    ("mul", 3, "PP"), ("mul", 3, "PM"), ("round", 3), ("attend", 3, 0), ("attend", 3, 1), ("attend", 3, 2),
    ("attend", 3, 3), ("mul", 4, "XM"), ("take_far", 4), ("mul", 4, "ZO"), ("mul", 4, "X2"), ("corner", 4),
    ("mul", 4, "PP"), ("mul", 4, "PM"), ("mul", 4, "CO"), ("round", 4), ("attend", 4, 0), ("attend", 4, 1),
    ("attend", 4, 2), ("attend", 4, 3),
)


def kernel(tok_hbm, wq_hbm, wk_hbm, wv_hbm, seg_ref, out, tok, acc, qkv, bias,
           load_sem, tok_sem, send_sem, recv_sem, *w):
    tokens = tok.shape[0]
    rows = wq_hbm.shape[0]
    half = rows // 2
    me = lax.axis_index("dp")
    head = lax.axis_index("head")
    zh, x, core = me // 8, lax.rem(me // 2, 4), lax.rem(me, 2)

    def device(dz, dx, dc):
        return (lax.rem(zh + dz, 2) * 4 + lax.rem(x + dx, 4)) * 2 + lax.rem(core + dc, 2)

    OWN, XP, XM, X2, ZO, PP, PM, CO = (0, 0), (0, 1), (0, 3), (0, 2), (1, 0), (1, 1), (1, 3), (1, 2)
    ALL = (OWN, XP, XM, X2, ZO, PP, PM, CO)
    BY_NAME = dict(OWN=OWN, XP=XP, XM=XM, X2=X2, ZO=ZO, PP=PP, PM=PM, CO=CO)
    to_left, to_right = (device(0, 3, 0), head), (device(0, 1, 0), head)
    partner, sibling = (device(1, 0, 0), head), (device(0, 0, 1), head)

    def apart(work):
        pl.when(me >= 0)(work)

    def part(c, pos, dc, first, count):
        start = pl.multiple_of(device(pos[0], pos[1], dc) * rows + first, 16)
        return w[c].at[pl.ds(start, count)]

    def send(c, pos, first, count, target, slot):
        ref = part(c, pos, 0, first, count)
        pltpu.make_async_remote_copy(
            src_ref=ref, dst_ref=ref, send_sem=send_sem.at[c, slot], recv_sem=recv_sem.at[c, slot],
            device_id=target, device_id_type=MESH).start()

    def pair(c, pos):
        send(c, pos, 0, rows, sibling, LANE + ALL.index(pos))

    def wait(c, pos, first, count, slot, dc=0):
        ref = part(c, pos, dc, first, count)
        pltpu.make_async_remote_copy(
            src_ref=ref, dst_ref=ref, send_sem=send_sem.at[c, slot], recv_sem=recv_sem.at[c, slot],
            device_id=sibling, device_id_type=MESH).wait_recv()

    def send_own(c):
        send(c, OWN, 0, rows, to_left, 0)
        send(c, OWN, 0, rows, to_right, 1)
        send(c, OWN, 0, rows, partner, 6)
        pair(c, OWN)

    def take_x(c):
        wait(c, XP, 0, rows, 0)
        send(c, XP, 0, half, to_left, 2)
        wait(c, XM, 0, rows, 1)
        send(c, XM, half, half, to_right, 3)
        if ROWS_X[c] < rows:
            send(c, XP, ROWS_X[c], rows - ROWS_X[c], partner, 8)
            send(c, XM, ROWS_X[c], rows - ROWS_X[c], partner, 9)
        pair(c, XP)
        pair(c, XM)

    def take_z(c):
        wait(c, ZO, 0, rows, 6)
        pair(c, ZO)

    def pieces(c):
        size = ROWS_X[c] // PIECES[c]
        return [(i * size, size) for i in range(PIECES[c])]

    def send_far(c):
        for i, (first, count) in enumerate(pieces(c)):
            send(c, ZO, first, count, to_left, (4, 10)[i])
            send(c, ZO, first, count, to_right, (5, 11)[i])

    def take_halves(c):
        wait(c, X2, 0, half, 2)
        wait(c, X2, half, half, 3)
        send(c, X2, 0, rows, partner, 7)
        pair(c, X2)

    def take_far(c):
        if ROWS_X[c] < rows:
            wait(c, PP, ROWS_X[c], rows - ROWS_X[c], 8)
            wait(c, PM, ROWS_X[c], rows - ROWS_X[c], 9)
        for i, (first, count) in enumerate(pieces(c)):
            on = rows - first if i == PIECES[c] - 1 else count
            wait(c, PP, first, count, (4, 10)[i])
            send(c, PP, first, on, sibling, (LANE + 5, 12)[i])
            wait(c, PM, first, count, (5, 11)[i])
            send(c, PM, first, on, sibling, (LANE + 6, 13)[i])

    def sibling_pieces(c, pos):
        slot = LANE + ALL.index(pos)
        if pos not in (PP, PM) or PIECES[c] == 1:
            return [(0, rows, slot)]
        size = ROWS_X[c] // PIECES[c]
        return [(0, size, slot), (size, rows - size, 12 if pos == PP else 13)]

    def take_corner(c):
        wait(c, CO, 0, rows, 7)
        pair(c, CO)

    started = set()

    def first_column(pos):
        return pl.multiple_of((lax.rem(zh + pos[0], 2) * 4 + lax.rem(x + pos[1], 4)) * 2 * rows, 1024)

    def project(c, names):
        positions = [BY_NAME[name] for name in names]
        for pos in positions:
            for first, count, slot in sibling_pieces(c, pos):
                wait(c, pos, first, count, slot, dc=1)
        columns = slice(0, w[c].shape[1])
        fresh = c not in started
        started.add(c)

        def multiply():
            total = None if fresh else acc[c % 2, :, columns]
            for pos in positions:
                at = pl.ds(first_column(pos), 2 * rows)
                part_sum = jnp.dot(tok[:, at], w[c][at], preferred_element_type=jnp.float32)
                total = part_sum if total is None else total + part_sum
            acc[c % 2, :, columns] = total

        apart(multiply)

    def round_chunk(c):
        def rounded():
            for h in range(CHUNKS[c][1]):
                qkv[CHUNKS[c][0] + h] = acc[c % 2, :, h * HEAD:(h + 1) * HEAD].astype(jnp.bfloat16)

        apart(rounded)

    def attend(c, ids):
        first, count = CHUNKS[c]
        tiles = tokens // TILE

        def tile_pair(i):
            work = [(first + h, i) for h in range(2)] if count == 2 else [(first, i), (first, tiles - 1 - i)]
            scores = [lax.dot_general(qkv[h, j * TILE:(j + 1) * TILE], qkv[0, :(j + 1) * TILE], (((1,), (1,)), ((), ())),
                                      preferred_element_type=jnp.float32)
                      + bias[j * TILE:(j + 1) * TILE, :(j + 1) * TILE] for h, j in work]
            weights = [jnp.exp2((s - jnp.max(s, axis=1, keepdims=True)) * EXP2_SCALE) for s in scores]
            for (h, j), p in zip(work, weights):
                total = jnp.sum(p, axis=1, keepdims=True)
                o = jnp.dot(p.astype(jnp.bfloat16), qkv[1, :(j + 1) * TILE], preferred_element_type=jnp.float32)
                out[j * TILE:(j + 1) * TILE, (h - 2) * HEAD:(h - 1) * HEAD] = (o / total).astype(jnp.bfloat16)

        def all_pairs():
            for i in ids:
                tile_pair(i)

        apart(all_pairs)

    def loads(c):
        at = pl.ds(pl.multiple_of(me * rows, rows), rows)
        if c == 0:
            return [pltpu.make_async_copy(wk_hbm, w[0].at[at, pl.ds(0, HEAD)], load_sem.at[0]),
                    pltpu.make_async_copy(wv_hbm, w[0].at[at, pl.ds(HEAD, HEAD)], load_sem.at[len(CHUNKS)])]
        first, count = CHUNKS[c]
        return [pltpu.make_async_copy(
            wq_hbm.at[:, pl.ds((first - 2) * HEAD, count * HEAD)], w[c].at[at], load_sem.at[c])]

    def tok_copy(name):
        at = pl.ds(first_column(BY_NAME[name]), 2 * rows)
        return pltpu.make_async_copy(tok_hbm.at[:, at], tok.at[:, at], tok_sem.at[ALL.index(BY_NAME[name])])

    for c in range(len(CHUNKS)):
        for copy in loads(c):
            copy.start()

    barrier = pltpu.get_barrier_semaphore()
    for target in (to_left, to_right, partner, sibling):
        pl.semaphore_signal(barrier, inc=1, device_id=target, device_id_type=MESH)
    pl.semaphore_wait(barrier, 4)

    begun = 0
    while ORDER[begun][0] == "own":
        for copy in loads(ORDER[begun][1]):
            copy.wait()
        send_own(ORDER[begun][1])
        begun += 1
    for c in range(begun, len(CHUNKS)):
        for copy in loads(c):
            copy.wait()
    for name in BY_NAME:
        tok_copy(name).start()

    def fill_mask():
        for i in range(tokens // HEAD):
            mine = jnp.transpose(jnp.broadcast_to(seg_ref[i:i + 1, :], (HEAD, HEAD)))
            for j in range((i * HEAD // TILE + 1) * TILE // HEAD):
                ok = mine == jnp.broadcast_to(seg_ref[j:j + 1, :], (HEAD, HEAD))
                t = lax.broadcasted_iota(jnp.int32, (HEAD, HEAD), 0) + i * HEAD
                u = lax.broadcasted_iota(jnp.int32, (HEAD, HEAD), 1) + j * HEAD
                bias[i * HEAD:(i + 1) * HEAD, j * HEAD:(j + 1) * HEAD] = jnp.where(
                    jnp.logical_and(ok, u <= t), jnp.float32(0.0), jnp.float32(NEGATIVE))

    apart(fill_mask)

    steps = dict(own=send_own, x=take_x, z=take_z, far=send_far, halves=take_halves, take_far=take_far, corner=take_corner,
                 mul=project, round=round_chunk, attend=attend)
    runs = []
    for step in ORDER[begun:]:
        if len(step) == 2:
            runs.append(step)
        elif runs and runs[-1][:2] == step[:2] and (
                len(runs[-1][2]) < MUL_RUN if step[0] == "mul" else sum(i + 1 for i in runs[-1][2]) + step[2] < TILE_RUN):
            runs[-1][2].append(step[2])
        else:
            runs.append((step[0], step[1], [step[2]]))
    seen = set()
    for run in runs:
        if run[0] == "mul":
            for name in run[2]:
                if name not in seen:
                    tok_copy(name).wait()
                    seen.add(name)
        steps[run[0]](*run[1:])

    for c in range(len(CHUNKS)):
        far = pieces(c) + [(0, 0)]
        rest = rows - ROWS_X[c]
        on = [sibling_pieces(c, pos) for pos in ALL]
        for slot, (pos, first, count) in enumerate(
                [(OWN, 0, rows), (OWN, 0, rows), (XP, 0, half), (XM, half, half), (ZO,) + far[0], (ZO,) + far[0],
                 (OWN, 0, rows), (X2, 0, rows), (XP, ROWS_X[c], rest), (XM, ROWS_X[c], rest), (ZO,) + far[1], (ZO,) + far[1]]
                + [(pos,) + (on[ALL.index(pos)] + [(0, 0)])[1][:2] for pos in (PP, PM)]
                + [(pos,) + on[i][0][:2] for i, pos in enumerate(ALL)]):
            if count > 0:
                ref = part(c, pos, 0, first, count)
                pltpu.make_async_remote_copy(
                    src_ref=ref, dst_ref=ref, send_sem=send_sem.at[c, slot], recv_sem=recv_sem.at[c, slot],
                    device_id=sibling, device_id_type=MESH).wait_send()


def body(tokens, w_query, key_weight, value_weight, segment_ids):
    seq, width = tokens.shape
    columns = w_query.shape[1]
    heads = columns // HEAD
    any_space = pl.BlockSpec(memory_space=pl.ANY)
    in_vmem = pl.BlockSpec(memory_space=pltpu.VMEM)
    return pl.pallas_call(
        kernel,
        out_shape=pltpu.VMEM((seq, columns), jnp.bfloat16),
        in_specs=[any_space] * 4 + [in_vmem],
        out_specs=in_vmem,
        scratch_shapes=[
            pltpu.VMEM((seq, width), jnp.bfloat16),
            pltpu.VMEM((2, seq, 2 * HEAD), jnp.float32),
            pltpu.VMEM((heads + 2, seq, HEAD), jnp.bfloat16),
            pltpu.VMEM((seq, seq), jnp.float32),
            pltpu.SemaphoreType.DMA((len(CHUNKS) + 1,)),
            pltpu.SemaphoreType.DMA((8,)),
            pltpu.SemaphoreType.DMA((len(CHUNKS), LANE + BLOCKS)),
            pltpu.SemaphoreType.DMA((len(CHUNKS), LANE + BLOCKS)),
        ] + [pltpu.VMEM((width, count * HEAD), jnp.bfloat16) for _, count in CHUNKS],
        compiler_params=pltpu.CompilerParams(
            collective_id=0, has_side_effects=True, vmem_limit_bytes=58 * 2**20),
        cost_estimate=pl.CostEstimate(
            flops=2 * seq * width * (columns + 2 * HEAD), bytes_accessed=40 * 2**20, transcendentals=heads * seq * seq),
    )(tokens, w_query, key_weight, value_weight, segment_ids.reshape(seq // HEAD, HEAD))


def solution(mesh):
    in_specs = (P("dp", None), P("dp", "head"), P("dp", "head"), P("dp", "head"), P("dp"))
    return jax.shard_map(body, mesh=mesh, in_specs=in_specs, out_specs=P("dp", "head"), check_vma=False)
```

time: 92.7 us -> 86.5 us (0.933)
  Pallas kernels: 89.5 us -> 85.1 us
  local copies, waits for them, and re-layouts: 3.08 us -> 1.32 us
    pallas_call x1, Pallas kernels: 89.5 us -> 85.1 us  [body(): pl.pallas_call(kernel, out_shape=pltpu.VMEM((seq, columns), jnp.bfloat16)...]
    unnamed x1, local copies, waits for them, and re-layouts: 3.08 us -> 1.32 us
where the time goes in v3:
time: 86.5 us; the launch traced here: 86.4 us
  Pallas kernels  85.1 us (98%)
  local copies, waits for them, and re-layouts  1.32 us (2%)
    pallas_call x1, Pallas kernels, body(): pl.pallas_call(kernel, out_shape=pltpu.VMEM((seq, columns), jnp.bfloat16)...  85.1 us

profile of v3, /device:TPU:1, one launch (start us, length us, event | category | flops | bytes accessed | tf_op | source)
XLA Modules:
  0.0 86.4 jit_solution(4148638475963270078)
XLA Ops:
  0.0 85.1 %shard_map.55 = bf16[1024,1024]{1,0:T(8,128)(2,1)S(1)} custom-call(bf16[1024,8192]{1,0:T(8,128)(2,1)} %tok_hbm.1, bf16[512,1024]{1,0:T(8,128)(2,1)} %wq_hbm.1, bf16[512,128]{1,0:T(8,128)(2,1)} %wk_hbm.1, bf16[512,128]{1,0:T(8,128)(2,1)} %wv_hbm.1, s32[8,128]{1,0:T(8,128)} %bitcast.1), custom_call_target="tpu_custom_call" | custom-call | flops 21474836480 | bytes 41943040 | tf_op jit(solution)/shard_map/pallas_call | solution.py:283
  85.1 1.3 %copy.7 = bf16[1024,1024]{1,0:T(8,128)(2,1)} copy(bf16[1024,1024]{1,0:T(8,128)(2,1)S(1)} %shard_map.55) | data formatting | bytes 4194304

commit v4 on v3

--- a/solution.py
+++ b/solution.py
@@ -14,7 +14,7 @@
 EXP2_SCALE = math.log2(math.e) / math.sqrt(HEAD)
 LANE = 14
 BLOCKS = 8
-ROWS_X = (416, 416, 416, 416, 416)
+ROWS_X = (400, 384, 448, 368, 480)
 PIECES = (1, 1, 1, 1, 1)
 MUL_RUN = 2
 TILE_RUN = 4
@@ -23,30 +23,31 @@
 CHUNKS = ((0, 2), (2, 2), (4, 2), (6, 2), (8, 2))
 
 ORDER = (
-    ("own", 0), ("own", 1), ("own", 2), ("mul", 0, "OWN"), ("mul", 1, "OWN"), ("own", 3), ("x", 0), ("z", 0),
-    ("mul", 0, "XP"), ("mul", 0, "XM"), ("mul", 0, "ZO"), ("x", 1), ("z", 1), ("mul", 1, "XP"),
-    ("mul", 1, "XM"), ("mul", 1, "ZO"), ("x", 2), ("z", 2), ("x", 3), ("z", 3), ("halves", 0),
-    ("mul", 0, "X2"), ("far", 0), ("halves", 1), ("mul", 1, "X2"), ("far", 1), ("halves", 2), ("far", 2),
-    ("halves", 3), ("corner", 0), ("own", 4), ("take_far", 0), ("mul", 0, "CO"), ("mul", 0, "PP"),
-    ("mul", 0, "PM"), ("far", 3), ("corner", 1), ("round", 0), ("mul", 2, "OWN"), ("take_far", 1),
-    ("mul", 2, "XP"), ("mul", 2, "XM"), ("mul", 1, "CO"), ("mul", 2, "ZO"), ("mul", 2, "X2"), ("mul", 1, "PP"),
-    ("mul", 1, "PM"), ("take_far", 2), ("round", 1), ("corner", 2), ("attend", 1, 0), ("attend", 1, 1),
-    ("attend", 1, 2), ("attend", 1, 3), ("mul", 2, "PP"), ("mul", 2, "CO"), ("mul", 2, "PM"), ("round", 2),
-    ("attend", 2, 0), ("attend", 2, 1), ("x", 4), ("corner", 3), ("attend", 2, 2), ("attend", 2, 3),
-    ("mul", 3, "OWN"), ("mul", 3, "XP"), ("mul", 3, "XM"), ("mul", 3, "ZO"), ("take_far", 3), ("mul", 3, "X2"),
-    ("mul", 3, "CO"), ("z", 4), ("far", 4), ("mul", 4, "OWN"), ("mul", 4, "XP"), ("halves", 4),
-    ("mul", 3, "PP"), ("mul", 3, "PM"), ("round", 3), ("attend", 3, 0), ("attend", 3, 1), ("attend", 3, 2),
-    ("attend", 3, 3), ("mul", 4, "XM"), ("take_far", 4), ("mul", 4, "ZO"), ("mul", 4, "X2"), ("corner", 4),
-    ("mul", 4, "PP"), ("mul", 4, "PM"), ("mul", 4, "CO"), ("round", 4), ("attend", 4, 0), ("attend", 4, 1),
-    ("attend", 4, 2), ("attend", 4, 3),
+    ("own", 0), ("own", 1), ("z", 0), ("x", 0), ("mul", 0, "XM"), ("own", 2), ("x", 1), ("halves", 0),
+    ("z", 1), ("mul", 0, "X2"), ("far", 1), ("far", 0), ("mul", 0, "XP"), ("halves", 1), ("x", 2), ("own", 3),
+    ("z", 2), ("corner", 0), ("take_far", 1), ("take_far", 0), ("mul", 0, "CO"), ("mul", 0, "OWN"),
+    ("mul", 1, "ZO"), ("mul", 1, "PP"), ("mul", 1, "X2"), ("mul", 0, "PM"), ("corner", 1), ("mul", 1, "XM"),
+    ("far", 2), ("mul", 0, "ZO"), ("mul", 0, "PP"), ("halves", 2), ("round", 0), ("mul", 1, "XP"),
+    ("mul", 2, "ZO"), ("mul", 2, "XM"), ("x", 3), ("mul", 1, "CO"), ("mul", 2, "XP"), ("mul", 1, "OWN"),
+    ("mul", 2, "OWN"), ("mul", 1, "PM"), ("round", 1), ("take_far", 2), ("mul", 3, "XP"), ("attend", 1, 0),
+    ("own", 4), ("attend", 1, 2), ("attend", 1, 3), ("z", 3), ("corner", 2), ("mul", 3, "XM"),
+    ("mul", 2, "PM"), ("attend", 1, 1), ("far", 3), ("mul", 2, "X2"), ("halves", 3), ("mul", 3, "OWN"),
+    ("mul", 2, "PP"), ("mul", 2, "CO"), ("round", 2), ("mul", 3, "ZO"), ("x", 4), ("attend", 2, 3), ("z", 4),
+    ("attend", 2, 0), ("attend", 2, 2), ("far", 4), ("mul", 4, "XM"), ("take_far", 3), ("mul", 3, "X2"),
+    ("mul", 4, "ZO"), ("attend", 2, 1), ("mul", 4, "XP"), ("halves", 4), ("mul", 4, "OWN"), ("corner", 3),
+    ("mul", 3, "PM"), ("mul", 3, "PP"), ("mul", 4, "X2"), ("mul", 3, "CO"), ("round", 3), ("attend", 3, 0),
+    ("attend", 3, 3), ("take_far", 4), ("attend", 3, 1), ("part", 4, "PM", 0), ("attend", 3, 2), ("corner", 4),
+    ("part", 4, "CO", 0), ("part", 4, "PP", 0), ("part", 4, "PP", 1), ("part", 4, "PM", 1),
+    ("part", 4, "CO", 1), ("round", 4), ("attend", 4, 3), ("attend", 4, 0), ("attend", 4, 2), ("attend", 4, 1),
 )
 
 
-def kernel(tok_hbm, wq_hbm, wk_hbm, wv_hbm, seg_ref, out, tok, acc, qkv, bias,
-           load_sem, tok_sem, send_sem, recv_sem, *w):
+def kernel(tok_hbm, wq_hbm, wk_hbm, wv_hbm, seg_hbm, out, tok, acc, qkv, bias, seg_ref,
+           load_sem, tok_sem, seg_sem, send_sem, recv_sem, *w):
     tokens = tok.shape[0]
     rows = wq_hbm.shape[0]
     half = rows // 2
+    last = len(CHUNKS) - 1
     me = lax.axis_index("dp")
     head = lax.axis_index("head")
     zh, x, core = me // 8, lax.rem(me // 2, 4), lax.rem(me, 2)
@@ -164,6 +165,19 @@
 
         apart(multiply)
 
+    def project_part(c, name, dc):
+        pos = BY_NAME[name]
+        if dc == 1:
+            for first, count, slot in sibling_pieces(c, pos):
+                wait(c, pos, first, count, slot, dc=1)
+        columns = slice(0, w[c].shape[1])
+        at = pl.ds(pl.multiple_of(device(pos[0], pos[1], dc) * rows, 512), rows)
+
+        def multiply():
+            acc[c % 2, :, columns] += jnp.dot(tok[:, at], w[c][at], preferred_element_type=jnp.float32)
+
+        apart(multiply)
+
     def round_chunk(c):
         def rounded():
             for h in range(CHUNKS[c][1]):
@@ -223,8 +237,11 @@
     for c in range(begun, len(CHUNKS)):
         for copy in loads(c):
             copy.wait()
+    seg_copy = pltpu.make_async_copy(seg_hbm, seg_ref, seg_sem)
+    seg_copy.start()
     for name in BY_NAME:
         tok_copy(name).start()
+    seg_copy.wait()
 
     def fill_mask():
         for i in range(tokens // HEAD):
@@ -238,27 +255,7 @@
 
     apart(fill_mask)
 
-    steps = dict(own=send_own, x=take_x, z=take_z, far=send_far, halves=take_halves, take_far=take_far, corner=take_corner,
-                 mul=project, round=round_chunk, attend=attend)
-    runs = []
-    for step in ORDER[begun:]:
-        if len(step) == 2:
-            runs.append(step)
-        elif runs and runs[-1][:2] == step[:2] and (
-                len(runs[-1][2]) < MUL_RUN if step[0] == "mul" else sum(i + 1 for i in runs[-1][2]) + step[2] < TILE_RUN):
-            runs[-1][2].append(step[2])
-        else:
-            runs.append((step[0], step[1], [step[2]]))
-    seen = set()
-    for run in runs:
-        if run[0] == "mul":
-            for name in run[2]:
-                if name not in seen:
-                    tok_copy(name).wait()
-                    seen.add(name)
-        steps[run[0]](*run[1:])
-
-    for c in range(len(CHUNKS)):
+    def drain(c):
         far = pieces(c) + [(0, 0)]
         rest = rows - ROWS_X[c]
         on = [sibling_pieces(c, pos) for pos in ALL]
@@ -273,6 +270,33 @@
                     src_ref=ref, dst_ref=ref, send_sem=send_sem.at[c, slot], recv_sem=recv_sem.at[c, slot],
                     device_id=sibling, device_id_type=MESH).wait_send()
 
+    steps = dict(own=send_own, x=take_x, z=take_z, far=send_far, halves=take_halves, take_far=take_far, corner=take_corner,
+                 mul=project, part=project_part, round=round_chunk, attend=attend)
+    runs = []
+    for step in ORDER[begun:]:
+        if len(step) != 3:
+            runs.append(step)
+        elif runs and runs[-1][:2] == step[:2] and (
+                len(runs[-1][2]) < MUL_RUN if step[0] == "mul" else sum(i + 1 for i in runs[-1][2]) + step[2] < TILE_RUN):
+            runs[-1][2].append(step[2])
+        else:
+            runs.append((step[0], step[1], [step[2]]))
+    seen = set()
+    drained = False
+    for run in runs:
+        if run[1] == last and run[0] in ("take_far", "corner") and not drained:
+            for c in range(last):
+                drain(c)
+            drained = True
+        if run[0] == "mul":
+            for name in run[2]:
+                if name not in seen:
+                    tok_copy(name).wait()
+                    seen.add(name)
+        steps[run[0]](*run[1:])
+
+    drain(last)
+
 
 def body(tokens, w_query, key_weight, value_weight, segment_ids):
     seq, width = tokens.shape
@@ -283,15 +307,17 @@
     return pl.pallas_call(
         kernel,
         out_shape=pltpu.VMEM((seq, columns), jnp.bfloat16),
-        in_specs=[any_space] * 4 + [in_vmem],
+        in_specs=[any_space] * 5,
         out_specs=in_vmem,
         scratch_shapes=[
             pltpu.VMEM((seq, width), jnp.bfloat16),
             pltpu.VMEM((2, seq, 2 * HEAD), jnp.float32),
             pltpu.VMEM((heads + 2, seq, HEAD), jnp.bfloat16),
             pltpu.VMEM((seq, seq), jnp.float32),
+            pltpu.VMEM((seq // HEAD, HEAD), jnp.int32),
             pltpu.SemaphoreType.DMA((len(CHUNKS) + 1,)),
             pltpu.SemaphoreType.DMA((8,)),
+            pltpu.SemaphoreType.DMA,
             pltpu.SemaphoreType.DMA((len(CHUNKS), LANE + BLOCKS)),
             pltpu.SemaphoreType.DMA((len(CHUNKS), LANE + BLOCKS)),
         ] + [pltpu.VMEM((width, count * HEAD), jnp.bfloat16) for _, count in CHUNKS],

time: 86.5 us -> 84.8 us (0.980)
  Pallas kernels: 85.1 us -> 83.4 us
    pallas_call x1, Pallas kernels: 85.1 us -> 83.4 us  [body(): pl.pallas_call(kernel, out_shape=pltpu.VMEM((seq, columns), jnp.bfloat16)...]
where the time goes in v4:
time: 84.8 us; the launch traced here: 84.7 us
  Pallas kernels  83.4 us (98%)
  local copies, waits for them, and re-layouts  1.32 us (2%)
    pallas_call x1, Pallas kernels, body(): pl.pallas_call(kernel, out_shape=pltpu.VMEM((seq, columns), jnp.bfloat16)...  83.4 us

profile of v4, /device:TPU:1, one launch (start us, length us, event | category | flops | bytes accessed | tf_op | source)
XLA Modules:
  0.0 84.7 jit_solution(1127314428043645524)
XLA Ops:
  0.0 83.4 %shard_map.55 = bf16[1024,1024]{1,0:T(8,128)(2,1)S(1)} custom-call(bf16[1024,8192]{1,0:T(8,128)(2,1)} %tok_hbm.1, bf16[512,1024]{1,0:T(8,128)(2,1)} %wq_hbm.1, bf16[512,128]{1,0:T(8,128)(2,1)} %wk_hbm.1, bf16[512,128]{1,0:T(8,128)(2,1)} %wv_hbm.1, s32[8,128]{1,0:T(8,128)} %bitcast.1), custom_call_target="tpu_custom_call" | custom-call | flops 21474836480 | bytes 41943040 | tf_op jit(solution)/shard_map/pallas_call | solution.py:307
  83.4 1.3 %copy.7 = bf16[1024,1024]{1,0:T(8,128)(2,1)} copy(bf16[1024,1024]{1,0:T(8,128)(2,1)S(1)} %shard_map.55) | data formatting | bytes 4194304

commit v5 on v4

--- a/solution.py
+++ b/solution.py
@@ -14,7 +14,7 @@
 EXP2_SCALE = math.log2(math.e) / math.sqrt(HEAD)
 LANE = 14
 BLOCKS = 8
-ROWS_X = (400, 384, 448, 368, 480)
+ROWS_X = (368, 400, 448, 384, 480)
 PIECES = (1, 1, 1, 1, 1)
 MUL_RUN = 2
 TILE_RUN = 4
@@ -23,22 +23,23 @@
 CHUNKS = ((0, 2), (2, 2), (4, 2), (6, 2), (8, 2))
 
 ORDER = (
-    ("own", 0), ("own", 1), ("z", 0), ("x", 0), ("mul", 0, "XM"), ("own", 2), ("x", 1), ("halves", 0),
-    ("z", 1), ("mul", 0, "X2"), ("far", 1), ("far", 0), ("mul", 0, "XP"), ("halves", 1), ("x", 2), ("own", 3),
-    ("z", 2), ("corner", 0), ("take_far", 1), ("take_far", 0), ("mul", 0, "CO"), ("mul", 0, "OWN"),
-    ("mul", 1, "ZO"), ("mul", 1, "PP"), ("mul", 1, "X2"), ("mul", 0, "PM"), ("corner", 1), ("mul", 1, "XM"),
-    ("far", 2), ("mul", 0, "ZO"), ("mul", 0, "PP"), ("halves", 2), ("round", 0), ("mul", 1, "XP"),
-    ("mul", 2, "ZO"), ("mul", 2, "XM"), ("x", 3), ("mul", 1, "CO"), ("mul", 2, "XP"), ("mul", 1, "OWN"),
-    ("mul", 2, "OWN"), ("mul", 1, "PM"), ("round", 1), ("take_far", 2), ("mul", 3, "XP"), ("attend", 1, 0),
-    ("own", 4), ("attend", 1, 2), ("attend", 1, 3), ("z", 3), ("corner", 2), ("mul", 3, "XM"),
-    ("mul", 2, "PM"), ("attend", 1, 1), ("far", 3), ("mul", 2, "X2"), ("halves", 3), ("mul", 3, "OWN"),
-    ("mul", 2, "PP"), ("mul", 2, "CO"), ("round", 2), ("mul", 3, "ZO"), ("x", 4), ("attend", 2, 3), ("z", 4),
-    ("attend", 2, 0), ("attend", 2, 2), ("far", 4), ("mul", 4, "XM"), ("take_far", 3), ("mul", 3, "X2"),
-    ("mul", 4, "ZO"), ("attend", 2, 1), ("mul", 4, "XP"), ("halves", 4), ("mul", 4, "OWN"), ("corner", 3),
-    ("mul", 3, "PM"), ("mul", 3, "PP"), ("mul", 4, "X2"), ("mul", 3, "CO"), ("round", 3), ("attend", 3, 0),
-    ("attend", 3, 3), ("take_far", 4), ("attend", 3, 1), ("part", 4, "PM", 0), ("attend", 3, 2), ("corner", 4),
-    ("part", 4, "CO", 0), ("part", 4, "PP", 0), ("part", 4, "PP", 1), ("part", 4, "PM", 1),
-    ("part", 4, "CO", 1), ("round", 4), ("attend", 4, 3), ("attend", 4, 0), ("attend", 4, 2), ("attend", 4, 1),
+    ("own", 0), ("own", 1), ("z", 0), ("x", 0), ("far", 0), ("own", 2), ("z", 1), ("take_far", 0),
+    ("halves", 0), ("x", 1), ("x", 2), ("mul", 0, "XM"), ("corner", 0), ("z", 2), ("mul", 1, "ZO"),
+    ("mul", 0, "PP"), ("halves", 1), ("far", 1), ("far", 2), ("mul", 1, "XP"), ("mul", 0, "XP"),
+    ("mul", 0, "CO"), ("halves", 2), ("mul", 1, "XM"), ("mul", 0, "PM"), ("mul", 1, "OWN"), ("mul", 0, "OWN"),
+    ("take_far", 1), ("mul", 0, "X2"), ("own", 3), ("mul", 0, "ZO"), ("round", 0), ("own", 4),
+    ("mul", 2, "XP"), ("corner", 1), ("mul", 1, "X2"), ("mul", 2, "X2"), ("mul", 2, "XM"), ("take_far", 2),
+    ("mul", 2, "OWN"), ("mul", 1, "PP"), ("mul", 1, "CO"), ("mul", 2, "PM"), ("mul", 1, "PM"), ("corner", 2),
+    ("mul", 2, "PP"), ("round", 1), ("x", 3), ("mul", 2, "CO"), ("attend", 1, 2), ("mul", 2, "ZO"),
+    ("attend", 1, 3), ("round", 2), ("attend", 1, 0), ("attend", 2, 3), ("attend", 1, 1), ("z", 3), ("far", 3),
+    ("attend", 2, 1), ("attend", 2, 0), ("mul", 4, "OWN"), ("mul", 3, "OWN"), ("halves", 3), ("z", 4),
+    ("x", 4), ("mul", 3, "XM"), ("far", 4), ("mul", 3, "ZO"), ("mul", 3, "XP"), ("attend", 2, 2),
+    ("mul", 4, "ZO"), ("take_far", 3), ("mul", 3, "X2"), ("mul", 4, "XP"), ("mul", 4, "XM"), ("halves", 4),
+    ("mul", 3, "PP"), ("corner", 3), ("mul", 3, "PM"), ("mul", 4, "X2"), ("mul", 3, "CO"), ("round", 3),
+    ("attend", 3, 0), ("attend", 3, 1), ("attend", 3, 2), ("take_far", 4), ("attend", 3, 3),
+    ("part", 4, "PP", 0), ("corner", 4), ("part", 4, "CO", 0), ("part", 4, "PM", 0), ("part", 4, "PP", 1),
+    ("part", 4, "PM", 1), ("part", 4, "CO", 1), ("round", 4), ("attend", 4, 1), ("attend", 4, 3),
+    ("attend", 4, 2), ("attend", 4, 0),
 )
 
 
@@ -219,13 +220,15 @@
         at = pl.ds(first_column(BY_NAME[name]), 2 * rows)
         return pltpu.make_async_copy(tok_hbm.at[:, at], tok.at[:, at], tok_sem.at[ALL.index(BY_NAME[name])])
 
-    for c in range(len(CHUNKS)):
-        for copy in loads(c):
-            copy.start()
+    for copy in loads(0):
+        copy.start()
 
     barrier = pltpu.get_barrier_semaphore()
     for target in (to_left, to_right, partner, sibling):
         pl.semaphore_signal(barrier, inc=1, device_id=target, device_id_type=MESH)
+    for c in range(1, len(CHUNKS)):
+        for copy in loads(c):
+            copy.start()
     pl.semaphore_wait(barrier, 4)
 
     begun = 0

time: 84.8 us -> 83.5 us (0.985)
  Pallas kernels: 83.4 us -> 82.1 us
    pallas_call x1, Pallas kernels: 83.4 us -> 82.1 us  [body(): pl.pallas_call(kernel, out_shape=pltpu.VMEM((seq, columns), jnp.bfloat16)...]
where the time goes in v5:
time: 83.5 us; the launch traced here: 83.4 us
  Pallas kernels  82.1 us (98%)
  local copies, waits for them, and re-layouts  1.32 us (2%)
    pallas_call x1, Pallas kernels, body(): pl.pallas_call(kernel, out_shape=pltpu.VMEM((seq, columns), jnp.bfloat16)...  82.1 us

profile of v5, /device:TPU:1, one launch (start us, length us, event | category | flops | bytes accessed | tf_op | source)
XLA Modules:
  0.0 83.4 jit_solution(18136072615602259518)
XLA Ops:
  0.0 82.1 %shard_map.55 = bf16[1024,1024]{1,0:T(8,128)(2,1)S(1)} custom-call(bf16[1024,8192]{1,0:T(8,128)(2,1)} %tok_hbm.1, bf16[512,1024]{1,0:T(8,128)(2,1)} %wq_hbm.1, bf16[512,128]{1,0:T(8,128)(2,1)} %wk_hbm.1, bf16[512,128]{1,0:T(8,128)(2,1)} %wv_hbm.1, s32[8,128]{1,0:T(8,128)} %bitcast.1), custom_call_target="tpu_custom_call" | custom-call | flops 21474836480 | bytes 41943040 | tf_op jit(solution)/shard_map/pallas_call | solution.py:310
  82.1 1.3 %copy.7 = bf16[1024,1024]{1,0:T(8,128)(2,1)} copy(bf16[1024,1024]{1,0:T(8,128)(2,1)S(1)} %shard_map.55) | data formatting | bytes 4194304

commit v6 on v5

--- a/solution.py
+++ b/solution.py
@@ -286,7 +286,12 @@
             runs.append((step[0], step[1], [step[2]]))
     seen = set()
     drained = False
+    parts_left = sum(run[0] == "part" for run in runs)
     for run in runs:
+        if run[0] == "part":
+            parts_left -= 1
+            if parts_left == 0:
+                drain(last)
         if run[1] == last and run[0] in ("take_far", "corner") and not drained:
             for c in range(last):
                 drain(c)
@@ -297,8 +302,6 @@
                     tok_copy(name).wait()
                     seen.add(name)
         steps[run[0]](*run[1:])
-
-    drain(last)
 
 
 def body(tokens, w_query, key_weight, value_weight, segment_ids):

time: 83.5 us -> 83.5 us (level)
  no operation moved by 1% of the time
where the time goes in v6:
time: 83.5 us; the launch traced here: 83.4 us
  Pallas kernels  82.1 us (98%)
  local copies, waits for them, and re-layouts  1.32 us (2%)
    pallas_call x1, Pallas kernels, body(): pl.pallas_call(kernel, out_shape=pltpu.VMEM((seq, columns), jnp.bfloat16)...  82.1 us

profile of v6, /device:TPU:1, one launch (start us, length us, event | category | flops | bytes accessed | tf_op | source)
XLA Modules:
  0.0 83.4 jit_solution(18158090562463335097)
XLA Ops:
  0.0 82.1 %shard_map.55 = bf16[1024,1024]{1,0:T(8,128)(2,1)S(1)} custom-call(bf16[1024,8192]{1,0:T(8,128)(2,1)} %tok_hbm.1, bf16[512,1024]{1,0:T(8,128)(2,1)} %wq_hbm.1, bf16[512,128]{1,0:T(8,128)(2,1)} %wk_hbm.1, bf16[512,128]{1,0:T(8,128)(2,1)} %wv_hbm.1, s32[8,128]{1,0:T(8,128)} %bitcast.1), custom_call_target="tpu_custom_call" | custom-call | flops 21474836480 | bytes 41943040 | tf_op jit(solution)/shard_map/pallas_call | solution.py:313
  82.1 1.3 %copy.7 = bf16[1024,1024]{1,0:T(8,128)(2,1)} copy(bf16[1024,1024]{1,0:T(8,128)(2,1)S(1)} %shard_map.55) | data formatting | bytes 4194304
